TPU v7x, 32 devices: a whole 2x2x4 slice. The times are simulated.
32 devices in a mesh: groups: 2 (over x), tok: 4 (over y, core), hid: 4 (over z).
Axes of the slice: x: 2, y: 2, z: 4, core: 2. Of those that a mesh axis runs over, the one named last changes fastest.
Arguments:
- tokens: bfloat16 [2048, 5376], P(('groups', 'tok'), 'hid'), parts along dimension 0, may hold values from -6 to 6
- w_query: bfloat16 [5376, 2048], P('tok', 'hid'), may hold values from -0.078125 to 0.078125
- key_weight: bfloat16 [5376, 1024], P('tok', 'hid'), may hold values from -0.078125 to 0.078125
- value_weight: bfloat16 [5376, 1024], P('tok', 'hid'), may hold values from -0.078125 to 0.078125
- w_out: bfloat16 [2048, 5376], P('tok', 'hid'), may hold values from -0.5 to 0.5
- query_norm_gain: float32 [128], replicated, may hold values from 0.5 to 2
- key_gain: float32 [128], replicated, may hold values from 0.5 to 2
- positions: int32 [2048], P('groups'), parts along dimension 0, may hold values from 0 to 131071, as said below
- grad_out: bfloat16 [2048, 5376], P(('groups', 'tok'), 'hid'), parts along dimension 0, may hold values from -6 to 6
Outputs:
- attn_out: bfloat16 [2048, 5376], P(('groups', 'tok'), 'hid'), parts along dimension 0
- grad_x: bfloat16 [2048, 5376], P(('groups', 'tok'), 'hid'), parts along dimension 0
- grad_wq: float32 [10752, 2048], P(('groups', 'tok'), 'hid'), parts along dimension 0
- key_weight_gradient: float32 [10752, 1024], P(('groups', 'tok'), 'hid'), parts along dimension 0
- value_weight_gradient: float32 [10752, 1024], P(('groups', 'tok'), 'hid'), parts along dimension 0
- grad_wo: float32 [4096, 5376], P(('groups', 'tok'), 'hid'), parts along dimension 0
There are 2 independent parts, one for each index of `groups`. A program takes and returns all parts, laid end to end along the dimension named above; an argument that names none is the same for every part. Nothing has to cross between parts.
Inputs may be any that keep to these rules, and one draw needn't show every extreme that they name: positions[t] is token t's position in its document: it rises by one from token to token and is 0 where a document begins; the first document begins before the window and its last token in the window has position 131071; at least one document begins inside the window.
All inputs are finite; a program needn't handle non-finite values.
Results may differ from a plain program's by a relative error of at most 0.02.
Values may be sent and summed in bfloat16 or wider, within the bound.
A program may use at most 192 MiB of HBM per device.

v0:
```python
import jax
import jax.numpy as jnp
from jax import lax
from jax.sharding import PartitionSpec as P

QUERY_HEADS = 16
KEY_VALUE_HEADS = 8
HEAD_SIZE = 128
WINDOW = 1024
TOK_DEV = 256
attn_scale = 168.0 ** (-0.5)
rope_base = 10000.0
norm_eps = 1e-06


def from_behind(value, axis, steps):
    count = lax.axis_size(axis)
    first, last = (max(0, -steps), min(count, count - steps))
    return lax.ppermute(value, axis, [(source, source + steps) for source in range(first, last)])


def rotary_tables(token_pos):
    half_dim = HEAD_SIZE // 2
    freqs = rope_base ** (-jnp.arange(half_dim, dtype=jnp.float32) * 2.0 / HEAD_SIZE)
    angles = token_pos.astype(jnp.float32)[:, None] * freqs[None, :]
    return (jnp.cos(angles), jnp.sin(angles))


def prepare_inputs(raw_values, gain_vector, cosine_table, sine_table):
    scaled = (
        raw_values
        * lax.rsqrt(jnp.mean(raw_values * raw_values, -1, keepdims=True) + norm_eps)
        * gain_vector
    )
    half_dim = scaled.shape[-1] // 2
    first_half = scaled[..., :half_dim]
    second_half = scaled[..., half_dim:]
    cos_rows = cosine_table[:, None, :]
    sin_rows = sine_table[:, None, :]
    return jnp.concatenate(
        [
            first_half * cos_rows - second_half * sin_rows,
            second_half * cos_rows + first_half * sin_rows,
        ],
        -1,
    )


def local(
    tokens, w_query, key_weight, value_weight, w_out, query_norm_gain, key_gain, positions, grad_out
):
    hidden_count = lax.axis_size("hid")
    block_index = lax.axis_index("tok")
    query_heads = QUERY_HEADS // hidden_count
    key_value_heads = KEY_VALUE_HEADS // hidden_count
    group_width = QUERY_HEADS // KEY_VALUE_HEADS
    reach = WINDOW // TOK_DEV
    span_rows = (reach + 1) * TOK_DEV
    leading_part = reach * TOK_DEV
    first_token = block_index * TOK_DEV
    query_cols = query_heads * HEAD_SIZE
    kv_cols = key_value_heads * HEAD_SIZE
    full_rows = lax.all_gather(tokens, "hid", axis=1, tiled=True)
    pieces = (
        lax.all_gather(w_query, "tok", axis=0, tiled=True),
        lax.all_gather(key_weight, "tok", axis=0, tiled=True),
        lax.all_gather(value_weight, "tok", axis=0, tiled=True),
    )
    columns = full_rows
    query_unnormed = jnp.dot(columns, pieces[0], preferred_element_type=jnp.float32)
    key_unnormed = jnp.dot(columns, pieces[1], preferred_element_type=jnp.float32)
    value_raw = jnp.dot(columns, pieces[2], preferred_element_type=jnp.float32)
    values_local = value_raw.astype(jnp.bfloat16)
    token_pos = lax.dynamic_slice_in_dim(positions, first_token, TOK_DEV, 0)
    cosine_table, sine_table = rotary_tables(token_pos)
    query_heads_raw = query_unnormed.reshape(TOK_DEV, query_heads, HEAD_SIZE)
    key_heads_raw = key_unnormed.reshape(TOK_DEV, key_value_heads, HEAD_SIZE)
    query_rows = (
        prepare_inputs(query_heads_raw, query_norm_gain, cosine_table, sine_table)
        .astype(jnp.bfloat16)
        .reshape(TOK_DEV, key_value_heads, group_width, HEAD_SIZE)
    )
    keys_local = prepare_inputs(key_heads_raw, key_gain, cosine_table, sine_table).astype(
        jnp.bfloat16
    )
    key_value = jnp.stack([keys_local.reshape(TOK_DEV, kv_cols), values_local], 0)
    blocks = [key_value]
    moving = key_value
    for turn_index in range(reach):
        moving = from_behind(moving, "tok", 1)
        blocks = [moving] + blocks
    window = jnp.concatenate(blocks, 1)
    key_window = window[0].reshape(span_rows, key_value_heads, HEAD_SIZE)
    value_window = window[1].reshape(span_rows, key_value_heads, HEAD_SIZE)
    query_index = first_token + jnp.arange(TOK_DEV, dtype=jnp.int32)
    key_index = first_token - leading_part + jnp.arange(span_rows, dtype=jnp.int32)
    padded_pos = jnp.pad(positions, (leading_part, 0))
    key_pos = lax.dynamic_slice_in_dim(padded_pos, first_token, span_rows, 0)
    distance = query_index[:, None] - key_index[None, :]
    allowed = (
        (key_index[None, :] >= 0)
        & (distance >= 0)
        & (distance < WINDOW)
        & (token_pos[:, None] - key_pos[None, :] == distance)
    )
    scores = (
        jnp.einsum("tkgd,ukd->kgtu", query_rows, key_window, preferred_element_type=jnp.float32)
        * attn_scale
    )
    weights = jnp.where(allowed[None, None], jnp.exp(scores), 0.0)
    probabilities = weights / jnp.sum(weights, -1, keepdims=True)
    rounded = probabilities.astype(jnp.bfloat16)
    attended = jnp.einsum(
        "kgtu,ukd->tkgd", rounded, value_window, preferred_element_type=jnp.float32
    )
    attended = attended.astype(jnp.bfloat16).reshape(TOK_DEV, query_cols)
    all_heads = lax.all_gather(attended, "hid", axis=1, tiled=True)
    columns = all_heads
    output = jnp.dot(
        columns,
        lax.all_gather(w_out, "tok", axis=0, tiled=True),
        preferred_element_type=jnp.float32,
    )
    attn_out = output.astype(jnp.bfloat16)
    partial_heads = jnp.einsum(
        "td,hd->th",
        grad_out,
        lax.all_gather(w_out, "tok", axis=0, tiled=True),
        preferred_element_type=jnp.float32,
    )
    attended_gradient = lax.psum_scatter(
        partial_heads.astype(jnp.bfloat16), "hid", scatter_dimension=1, tiled=True
    )
    attended_gradient = attended_gradient.reshape(TOK_DEV, key_value_heads, group_width, HEAD_SIZE)
    columns = all_heads
    grad_wo = lax.psum_scatter(
        jnp.einsum("th,td->hd", columns, grad_out, preferred_element_type=jnp.float32).astype(
            jnp.bfloat16
        ),
        "tok",
        scatter_dimension=0,
        tiled=True,
    ).astype(jnp.float32)
    grad_probs = jnp.einsum(
        "tkgd,ukd->kgtu", attended_gradient, value_window, preferred_element_type=jnp.float32
    )
    grad_scores = (
        attn_scale
        * probabilities
        * (grad_probs - jnp.sum(probabilities * grad_probs, -1, keepdims=True))
    )
    grad_scores = grad_scores.astype(jnp.bfloat16)
    grad_queries = jnp.einsum(
        "kgtu,ukd->tkgd", grad_scores, key_window, preferred_element_type=jnp.float32
    )
    keys_gradient = jnp.einsum(
        "kgtu,tkgd->ukd", grad_scores, query_rows, preferred_element_type=jnp.float32
    )
    values_gradient = jnp.einsum(
        "kgtu,tkgd->ukd", rounded, attended_gradient, preferred_element_type=jnp.float32
    )
    grad_window = jnp.stack(
        [keys_gradient.reshape(span_rows, kv_cols), values_gradient.reshape(span_rows, kv_cols)], 0
    )
    grad_kv = grad_window[:, :TOK_DEV]
    for turn_index in range(1, reach + 1):
        grad_kv = (
            from_behind(grad_kv.astype(jnp.bfloat16), "tok", -1).astype(grad_kv.dtype)
            + grad_window[:, turn_index * TOK_DEV : (turn_index + 1) * TOK_DEV]
        )
    _, query_pull = jax.vjp(
        lambda raw_values: prepare_inputs(raw_values, query_norm_gain, cosine_table, sine_table),
        query_heads_raw,
    )
    _, key_pullback = jax.vjp(
        lambda raw_values: prepare_inputs(raw_values, key_gain, cosine_table, sine_table),
        key_heads_raw,
    )
    query_back = (
        query_pull(grad_queries.reshape(TOK_DEV, query_heads, HEAD_SIZE))[0]
        .astype(jnp.bfloat16)
        .reshape(TOK_DEV, query_cols)
    )
    key_backward = (
        key_pullback(grad_kv[0].reshape(TOK_DEV, key_value_heads, HEAD_SIZE))[0]
        .astype(jnp.bfloat16)
        .reshape(TOK_DEV, kv_cols)
    )
    value_backward = grad_kv[1].astype(jnp.bfloat16)
    pieces = (
        lax.all_gather(w_query, "tok", axis=0, tiled=True),
        lax.all_gather(key_weight, "tok", axis=0, tiled=True),
        lax.all_gather(value_weight, "tok", axis=0, tiled=True),
    )
    block_rows = jnp.einsum("tc,dc->td", query_back, pieces[0], preferred_element_type=jnp.float32)
    block_rows = block_rows + jnp.einsum(
        "tc,dc->td", key_backward, pieces[1], preferred_element_type=jnp.float32
    )
    block_rows = block_rows + jnp.einsum(
        "tc,dc->td", value_backward, pieces[2], preferred_element_type=jnp.float32
    )
    grad_x = lax.psum_scatter(
        block_rows.astype(jnp.bfloat16), "hid", scatter_dimension=1, tiled=True
    )
    joined = jnp.concatenate([query_back, key_backward, value_backward], 1)
    columns = full_rows
    inputs_gradient = lax.psum_scatter(
        jnp.einsum("td,tc->dc", columns, joined, preferred_element_type=jnp.float32).astype(
            jnp.bfloat16
        ),
        "tok",
        scatter_dimension=0,
        tiled=True,
    ).astype(jnp.float32)
    grad_wq = inputs_gradient[:, :query_cols]
    key_weight_gradient = inputs_gradient[:, query_cols : query_cols + kv_cols]
    value_weight_gradient = inputs_gradient[:, query_cols + kv_cols :]
    return (attn_out, grad_x, grad_wq, key_weight_gradient, value_weight_gradient, grad_wo)


def solution(mesh):
    return jax.shard_map(
        local,
        mesh=mesh,
        in_specs=(
            P(("groups", "tok"), "hid"),
            P("tok", "hid"),
            P("tok", "hid"),
            P("tok", "hid"),
            P("tok", "hid"),
            P(),
            P(),
            P("groups"),
            P(("groups", "tok"), "hid"),
        ),
        out_specs=(
            P(("groups", "tok"), "hid"),
            P(("groups", "tok"), "hid"),
            P(("groups", "tok"), "hid"),
            P(("groups", "tok"), "hid"),
            P(("groups", "tok"), "hid"),
            P(("groups", "tok"), "hid"),
        ),
        check_vma=False,
    )
```

profile of v0, /device:TPU:0, one launch (start us, length us, event | category | flops | bytes accessed | tf_op | source)
XLA Modules:
  0.0 533.1 jit_solution(8596791121754949615)
XLA Ops:
  12.1 57.2 %all-gather.7.cloned.1.call-done = bf16[256,5376]{0,1:T(8,128)(2,1)} async-done(((bf16[256,1344]{0,1:T(8,128)(2,1)}), bf16[256,5376]{0,1:T(8,128)(2,1)}) %all-gather.7.cloned.1.call-update) | async-done | bytes 2752528 | tf_op jit(solution)/shard_map/all_gather | solution.py:63
  69.3 26.6 %all-gather.9.cloned.1.call-done = bf16[5376,256]{1,0:T(8,128)(2,1)} async-done(((bf16[1344,256]{1,0:T(8,128)(2,1)}), bf16[5376,256]{1,0:T(8,128)(2,1)}) %all-gather.9.cloned.1.call-update) | async-done | bytes 2752528 | tf_op jit(solution)/shard_map/all_gather | solution.py:66
  95.9 3.8 multiply_reduce_fusion.3
  103.0 20.9 %all-gather.11.cloned.1.call-done = bf16[5376,256]{1,0:T(8,128)(2,1)} async-done(((bf16[1344,256]{1,0:T(8,128)(2,1)}), bf16[5376,256]{1,0:T(8,128)(2,1)}) %all-gather.11.cloned.1.call-update) | async-done | bytes 2752528 | tf_op jit(solution)/shard_map/all_gather | solution.py:67
  131.3 4.9 collective-permute-start.1
  137.0 12.5 %collective-permute-start.2 = (bf16[2,256,256]{2,1,0:T(8,128)(2,1)}, bf16[2,256,256]{2,1,0:T(8,128)(2,1)}, u32[]{:S(2)}, u32[]{:S(2)}) collective-permute-start(bf16[2,256,256]{2,1,0:T(8,128)(2,1)} %collective-permute-done.1), channel_id=1, source_target_pairs={{0,4},{4,8},{8,12},{1,5},{5,9},{9,13},{2,6},{6,10},{10,14},{3,7},{... | collective-permute-start | bytes 786440 | tf_op jit(solution)/shard_map/ppermute | solution.py:19
  150.3 12.2 %collective-permute-start.3 = (bf16[2,256,256]{2,1,0:T(8,128)(2,1)}, bf16[2,256,256]{2,1,0:T(8,128)(2,1)S(1)}, u32[]{:S(2)}, u32[]{:S(2)}) collective-permute-start(bf16[2,256,256]{2,1,0:T(8,128)(2,1)} %collective-permute-done.2), channel_id=1, source_target_pairs={{0,4},{4,8},{8,12},{1,5},{5,9},{9,13},{2,6},{6,10},{10,14},{3,7},{... | collective-permute-start | bytes 786440 | tf_op jit(solution)/shard_map/ppermute | solution.py:19
  170.9 5.3 %convolution_convert_fusion.3 = bf16[256,2048]{1,0:T(8,128)(2,1)} fusion(bf16[256,1344]{0,1:T(8,128)(2,1)S(1)} %copy-done, bf16[2048,1344]{0,1:T(8,128)(2,1)} %all-gather.17.cloned.1.call-done), kind=kOutput, calls=%fused_computation.23 | convolution fusion | flops 1409810432 | bytes 7241728 | tf_op jit(solution)/shard_map/td,hd->th/dot_general | solution.py:125
  185.7 3.0 copy.117
  188.7 29.4 %all-gather.13.cloned.1.call-done = bf16[5376,512]{1,0:T(8,128)(2,1)} async-done(((bf16[1344,512]{1,0:T(8,128)(2,1)}), bf16[5376,512]{1,0:T(8,128)(2,1)}) %all-gather.13.cloned.1.call-update) | async-done | bytes 5505040 | tf_op jit(solution)/shard_map/all_gather | solution.py:65
  218.1 5.0 fusion.53
  225.9 22.1 %reduce-scatter.7.cloned.1.call-done = bf16[256,512]{1,0:T(8,128)(2,1)} async-done(((bf16[256,2048]{1,0:T(8,128)(2,1)}), bf16[256,512]{1,0:T(8,128)(2,1)}) %reduce-scatter.7.cloned.1.call-update) | async-done | bytes 262160 | tf_op jit(solution)/shard_map/reduce_scatter | solution.py:131
  249.1 3.2 fusion.19
  252.3 7.2 %fusion.2 = (f32[2,2,256]{2,1,0:T(2,128)S(1)}, f32[2,2,256,1280]{2,3,1,0:T(8,128)}) fusion(f32[2,1280,256,2]{2,1,3,0:T(8,128)} %fusion.19, bf16[1280,2,128,1]{0,2,3,1:T(8,128)(2,1)S(1)} %copy-done.14, pred[256,1280]{0,1:T(8,128)(4,1)S(1)} %copy-done.34, bf16[256,2,2,64]{3,0,2,1:T(8,128)(2,1)S(1)} %bitcast.103, bf16[256,2,2,64]{3,0,2,1:T(8,128)(2,1)S(1)} %bitcast.105), kind=kOutput, calls=%fused_computation.8 | convolution fusion | flops 342623488 | bytes 11735040 | tf_op jit(solution)/shard_map/div | solution.py:111
  259.5 3.8 fusion.14
  263.3 26.7 %all-gather.15.cloned.1.call-done = bf16[256,2048]{0,1:T(8,128)(2,1)} async-done(((bf16[256,512]{0,1:T(8,128)(2,1)}), bf16[256,2048]{0,1:T(8,128)(2,1)}) %all-gather.15.cloned.1.call-update) | async-done | bytes 1048592 | tf_op jit(solution)/shard_map/all_gather | solution.py:117
  290.0 5.2 convolution_convert_fusion.1
  295.5 4.8 fusion.4
  301.4 4.5 fusion.7
  314.2 3.2 collective-permute-done.5
  322.5 10.5 %collective-permute-done.6 = bf16[2,256,256]{1,2,0:T(8,128)(2,1)} collective-permute-done((bf16[2,256,256]{1,2,0:T(8,128)(2,1)}, bf16[2,256,256]{1,2,0:T(8,128)(2,1)}, u32[]{:S(2)}, u32[]{:S(2)}) %collective-permute-start.6) | collective-permute-done | bytes 262176 | tf_op jit(solution)/shard_map/ppermute | solution.py:19
  339.0 9.6 %collective-permute-done.7 = bf16[2,256,256]{1,2,0:T(8,128)(2,1)} collective-permute-done((bf16[2,256,256]{1,2,0:T(8,128)(2,1)}, bf16[2,256,256]{1,2,0:T(8,128)(2,1)}, u32[]{:S(2)}, u32[]{:S(2)}) %collective-permute-start.7) | collective-permute-done | bytes 262176 | tf_op jit(solution)/shard_map/ppermute | solution.py:19
  352.2 7.7 %fusion = bf16[5376,1024]{0,1:T(8,128)(2,1)} fusion(bf16[256,5376]{0,1:T(8,128)(2,1)} %all-gather.7.cloned.1.call-done, bf16[256,256]{1,0:T(8,128)(2,1)S(1)} %copy.109, bf16[256,256]{1,0:T(8,128)(2,1)S(1)} %copy.108, bf16[256,512]{1,0:T(8,128)(2,1)S(1)} %bitcast.102), kind=kOutput, calls=%fused_computation.1 | convolution fusion | flops 2825650176 | bytes 14286848 | tf_op jit(solution)/shard_map/td,tc->dc/dot_general | solution.py:208
  359.9 14.7 %copy.133 = bf16[5376,1024]{1,0:T(8,128)(2,1)} copy(bf16[5376,1024]{0,1:T(8,128)(2,1)} %fusion) | data formatting | bytes 22020096
  375.5 4.3 fusion.47
  385.5 5.5 %convolution_convert_fusion.2 = bf16[256,1344]{0,1:T(8,128)(2,1)} fusion(bf16[2048,1344]{0,1:T(8,128)(2,1)} %all-gather.17.cloned.1.call-done, bf16[256,2048]{0,1:T(8,128)(2,1)S(1)} %copy-done.26), kind=kOutput, calls=%fused_computation.22 | convolution fusion | flops 1409630208 | bytes 7241728 | tf_op jit(solution)/shard_map/dot_general | solution.py:119
  391.0 3.6 convert_element_type.111
  394.6 74.7 %reduce-scatter.13.cloned.1.call-done = bf16[1344,1024]{1,0:T(8,128)(2,1)} async-done(((bf16[5376,1024]{1,0:T(8,128)(2,1)}), bf16[1344,1024]{1,0:T(8,128)(2,1)}) %reduce-scatter.13.cloned.1.call-update) | async-done | bytes 2752528
  469.3 4.6 copy.134
  473.9 3.1 slice.82
  477.0 3.8 copy.110
  487.8 38.4 %reduce-scatter.9.cloned.1.call-done = bf16[256,1344]{0,1:T(8,128)(2,1)} async-done(((bf16[256,5376]{0,1:T(8,128)(2,1)}), bf16[256,1344]{0,1:T(8,128)(2,1)}) %reduce-scatter.9.cloned.1.call-update) | async-done | bytes 688144 | tf_op jit(solution)/shard_map/reduce_scatter | solution.py:202
  (173 shorter events, 76.1 us)
Async XLA Ops:
  7.2 163.8 %copy-start = (bf16[256,1344]{0,1:T(8,128)(2,1)S(1)}, bf16[256,1344]{0,1:T(8,128)(2,1)}, u32[]{:S(2)}) copy-start(bf16[256,1344]{0,1:T(8,128)(2,1)} %param.17) | copy-start | bytes 2064388
  7.2 62.1 %all-gather.7.cloned.1.call-start = ((), (), s32[]{:S(2)}) async-start(), calls=%async_computation.4 | async-start | bytes 3440640 | tf_op jit(solution)/shard_map/all_gather | solution.py:63
  7.9 88.0 %all-gather.9.cloned.1.call-start = ((), (), s32[]{:S(2)}) async-start(), calls=%async_computation.5 | async-start | bytes 3440640 | tf_op jit(solution)/shard_map/all_gather | solution.py:66
  8.7 115.2 %all-gather.11.cloned.1.call-start = ((), (), s32[]{:S(2)}) async-start(), calls=%async_computation.6 | async-start | bytes 3440640 | tf_op jit(solution)/shard_map/all_gather | solution.py:67
  9.4 161.5 %all-gather.17.cloned.1.call-start = ((), (), s32[]{:S(2)}) async-start(), calls=%async_computation.9 | async-start | bytes 6881280 | tf_op jit(solution)/shard_map/all_gather | solution.py:121
  10.0 208.1 %all-gather.13.cloned.1.call-start = ((), (), s32[]{:S(2)}) async-start(), calls=%async_computation.7 | async-start | bytes 6881280 | tf_op jit(solution)/shard_map/all_gather | solution.py:65
  10.6 237.4 %reduce-scatter.7.cloned.1.call-start = ((), (), s32[]{:S(2)}) async-start(), calls=%async_computation.10 | async-start | bytes 1310720 | tf_op jit(solution)/shard_map/reduce_scatter | solution.py:131
  12.1 88.4 %copy-start.38 = (f32[128]{0:T(128)S(1)}, f32[128]{0:T(128)}, u32[]{:S(2)}) copy-start(f32[128]{0:T(128)} %param.15) | copy-start | bytes 1540
  69.3 54.6 %copy-start.2 = (bf16[256,5376]{0,1:T(8,128)(2,1)S(1)}, bf16[256,5376]{0,1:T(8,128)(2,1)}, u32[]{:S(2)}) copy-start(bf16[256,5376]{0,1:T(8,128)(2,1)} %all-gather.7.cloned.1.call-done) | copy-start | bytes 8257540
  127.3 3.3 collective-permute-start
  131.3 5.8 %collective-permute-start.1 = (bf16[2,256,256]{2,1,0:T(8,128)(2,1)S(1)}, bf16[2,256,256]{2,1,0:T(8,128)(2,1)}, u32[]{:S(2)}, u32[]{:S(2)}) collective-permute-start(bf16[2,256,256]{2,1,0:T(8,128)(2,1)S(1)} %collective-permute-done), channel_id=1, source_target_pairs={{0,4},{4,8},{8,12},{1,5},{5,9},{9,13},{2,6},{6,10},{10,14},{3,7},{... | collective-permute-start | bytes 786440 | tf_op jit(solution)/shard_map/ppermute | solution.py:19
  137.0 13.2 %collective-permute-start.2 = (bf16[2,256,256]{2,1,0:T(8,128)(2,1)}, bf16[2,256,256]{2,1,0:T(8,128)(2,1)}, u32[]{:S(2)}, u32[]{:S(2)}) collective-permute-start(bf16[2,256,256]{2,1,0:T(8,128)(2,1)} %collective-permute-done.1), channel_id=1, source_target_pairs={{0,4},{4,8},{8,12},{1,5},{5,9},{9,13},{2,6},{6,10},{10,14},{3,7},{... | collective-permute-start | bytes 786440 | tf_op jit(solution)/shard_map/ppermute | solution.py:19
  150.3 14.3 %collective-permute-start.3 = (bf16[2,256,256]{2,1,0:T(8,128)(2,1)}, bf16[2,256,256]{2,1,0:T(8,128)(2,1)S(1)}, u32[]{:S(2)}, u32[]{:S(2)}) collective-permute-start(bf16[2,256,256]{2,1,0:T(8,128)(2,1)} %collective-permute-done.2), channel_id=1, source_target_pairs={{0,4},{4,8},{8,12},{1,5},{5,9},{9,13},{2,6},{6,10},{10,14},{3,7},{... | collective-permute-start | bytes 786440 | tf_op jit(solution)/shard_map/ppermute | solution.py:19
  176.3 113.7 %all-gather.15.cloned.1.call-start = ((), (), s32[]{:S(2)}) async-start(), calls=%async_computation.8 | async-start | bytes 1310720 | tf_op jit(solution)/shard_map/all_gather | solution.py:117
  188.7 36.2 %copy-start.37 = (f32[128]{0:T(128)S(1)}, f32[128]{0:T(128)}, u32[]{:S(2)}) copy-start(f32[128]{0:T(128)} %param.14) | copy-start | bytes 1540
  224.3 24.8 %copy-start.3 = (f32[256,4,128]{2,1,0:T(4,128)}, f32[256,4,128]{2,1,0:T(4,128)S(1)}, u32[]{:S(2)}) copy-start(f32[256,4,128]{2,1,0:T(4,128)S(1)} %reshape.224) | copy-start | bytes 1572868
  224.3 24.8 %copy-start.6 = (bf16[1280,2,128]{2,1,0:T(2,128)(2,1)S(1)}, bf16[1280,2,128]{2,1,0:T(2,128)(2,1)}, u32[]{:S(2)}) copy-start(bf16[1280,2,128]{2,1,0:T(2,128)(2,1)} %reshape_squeeze.9) | copy-start | bytes 1966084
  224.9 24.2 %copy-start.27 = (f32[256,4]{1,0:T(8,128)}, f32[256,4]{1,0:T(8,128)S(1)}, u32[]{:S(2)}) copy-start(f32[256,4]{1,0:T(8,128)S(1)} %copy.90) | copy-start | bytes 12292
  263.3 127.7 %reduce-scatter.11.cloned.1.call-start = ((), (), s32[]{:S(2)}) async-start(), calls=%async_computation.12 | async-start | bytes 6881280 | tf_op jit(solution)/shard_map/reduce_scatter | solution.py:136
  295.3 174.0 %reduce-scatter.13.cloned.1.call-start = ((), (), s32[]{:S(2)}) async-start(), calls=%async_computation.13 | async-start | bytes 13762560
  306.0 3.6 collective-permute-start.4
  310.4 7.1 %collective-permute-start.5 = (bf16[2,256,256]{1,2,0:T(8,128)(2,1)}, bf16[2,256,256]{1,2,0:T(8,128)(2,1)}, u32[]{:S(2)}, u32[]{:S(2)}) collective-permute-start(bf16[2,256,256]{1,2,0:T(8,128)(2,1)} %fusion.29), channel_id=1, source_target_pairs={{4,0},{8,4},{12,8},{5,1},{9,5},{13,9},{6,2},{10,6},{14,10},{7,3},{... | collective-permute-start | bytes 786440 | tf_op jit(solution)/shard_map/ppermute | solution.py:19
  312.2 8.3 %copy-start.23 = (f32[256,64]{1,0:T(8,128)S(1)}, f32[256,64]{1,0:T(8,128)}, u32[]{:S(2)}) copy-start(f32[256,64]{1,0:T(8,128)} %copy-done.21) | copy-start | bytes 196612
  314.2 7.5 %copy-start.4 = (f32[256,4,128]{2,1,0:T(4,128)S(1)}, f32[256,4,128]{2,1,0:T(4,128)}, u32[]{:S(2)}) copy-start(f32[256,4,128]{2,1,0:T(4,128)} %copy-done.3) | copy-start | bytes 1572868
  319.1 13.9 %collective-permute-start.6 = (bf16[2,256,256]{1,2,0:T(8,128)(2,1)}, bf16[2,256,256]{1,2,0:T(8,128)(2,1)}, u32[]{:S(2)}, u32[]{:S(2)}) collective-permute-start(bf16[2,256,256]{1,2,0:T(8,128)(2,1)} %fusion.32), channel_id=1, source_target_pairs={{4,0},{8,4},{12,8},{5,1},{9,5},{13,9},{6,2},{10,6},{14,10},{7,3},{... | collective-permute-start | bytes 786440 | tf_op jit(solution)/shard_map/ppermute | solution.py:19
  320.8 15.4 %copy-start.28 = (f32[256,4]{1,0:T(8,128)S(1)}, f32[256,4]{1,0:T(8,128)}, u32[]{:S(2)}) copy-start(f32[256,4]{1,0:T(8,128)} %copy-done.27) | copy-start | bytes 12292
  334.7 13.9 %collective-permute-start.7 = (bf16[2,256,256]{1,2,0:T(8,128)(2,1)}, bf16[2,256,256]{1,2,0:T(8,128)(2,1)}, u32[]{:S(2)}, u32[]{:S(2)}) collective-permute-start(bf16[2,256,256]{1,2,0:T(8,128)(2,1)} %fusion.24), channel_id=1, source_target_pairs={{4,0},{8,4},{12,8},{5,1},{9,5},{13,9},{6,2},{10,6},{14,10},{7,3},{... | collective-permute-start | bytes 786440 | tf_op jit(solution)/shard_map/ppermute | solution.py:19
  338.2 11.4 %copy-start.9 = (bf16[256,4,128]{2,1,0:T(4,128)(2,1)}, bf16[256,4,128]{2,1,0:T(4,128)(2,1)S(1)}, u32[]{:S(2)}) copy-start(bf16[256,4,128]{2,1,0:T(4,128)(2,1)S(1)} %fusion.21) | copy-start | bytes 786436
  338.2 11.6 %copy-start.32 = (f32[256,64]{0,1:T(8,128)S(1)}, f32[256,64]{0,1:T(8,128)}, u32[]{:S(2)}) copy-start(f32[256,64]{0,1:T(8,128)} %copy.86) | copy-start | bytes 196612
  349.6 10.2 %copy-start.12 = (f32[2,256,256]{1,2,0:T(8,128)}, f32[2,256,256]{1,2,0:T(8,128)S(1)}, u32[]{:S(2)}) copy-start(f32[2,256,256]{1,2,0:T(8,128)S(1)} %fusion.33) | copy-start | bytes 1572868
  374.6 151.6 %reduce-scatter.9.cloned.1.call-start = ((), (), s32[]{:S(2)}) async-start(), calls=%async_computation.11 | async-start | bytes 3440640 | tf_op jit(solution)/shard_map/reduce_scatter | solution.py:202
  483.4 42.8 %copy-start.1 = (bf16[256,1344]{0,1:T(8,128)(2,1)S(1)}, bf16[256,1344]{0,1:T(8,128)(2,1)}, u32[]{:S(2)}) copy-start(bf16[256,1344]{0,1:T(8,128)(2,1)} %param.17) | copy-start | bytes 2064388
  (25 other events, 62.2 us)
Sparse Core Ops, SparseCore 0:
  9.6 59.6 all-gather.6
  70.9 25.0 all-gather.8
  97.5 26.3 all-gather.10
  125.3 45.5 all-gather.16
  172.3 45.6 all-gather.12
  220.8 27.1 reduce-scatter.6
  263.4 26.5 all-gather.14
  295.4 59.1 reduce-scatter.10
  374.7 94.5 reduce-scatter.12
  472.1 54.1 reduce-scatter.8
where the time goes:
time: 535 us; the launch traced here: 533 us
  waiting for transfers between devices  328 us (61%)
  local copies, waits for them, and re-layouts  63.6 us (12%)
  matrix products  63.2 us (12%)
  starting transfers between devices  38.1 us (7%)
  other arithmetic  25.4 us (5%)
  between operations  14.9 us (3%)
    unnamed x11, waiting for transfers between devices  77.9 us
    all_gather x1, waiting for transfers between devices, local(): full_rows = lax.all_gather(tokens, 'hid', axis=1, tiled=True)  57.2 us
    unnamed x90, local copies, waits for them, and re-layouts  41.8 us
    reduce_scatter x1, waiting for transfers between devices, local(): lax.psum_scatter(block_rows.astype(jnp.bfloat16), 'hid', scatter_dimensio...  38.4 us
    ppermute x8, starting transfers between devices, from_behind(): lax.ppermute(value, axis, [(source, source + steps) for source in range(f...  37 us
    all_gather x1, waiting for transfers between devices, local(): lax.all_gather(w_query, 'tok', axis=0, tiled=True)  29.4 us
    ppermute x8, waiting for transfers between devices, from_behind(): lax.ppermute(value, axis, [(source, source + steps) for source in range(f...  28.1 us
    all_gather x1, waiting for transfers between devices, local(): all_heads = lax.all_gather(attended, 'hid', axis=1, tiled=True)  26.7 us
  transfers between devices with their start and end apart: 18, of which 16 were waited for; matrix products, arithmetic and copies ran while one was open for 24% of the time, Pallas kernels for 0%

commit v1 on v0

--- a/solution.py
+++ b/solution.py
@@ -11,6 +11,27 @@
 attn_scale = 168.0 ** (-0.5)
 rope_base = 10000.0
 norm_eps = 1e-06
+
+
+def draw_islands_on(block_here, axis_k):
+    block_here = jnp.moveaxis(block_here, 0, axis_k)
+    z_new = block_here.shape
+    return block_here.reshape(
+        *z_new[:axis_k], z_new[axis_k] * z_new[axis_k + 1], *z_new[axis_k + 2 :]
+    )
+
+
+def see_clusters(shard_in, peer_axis):
+    k_all = lax.axis_size(peer_axis)
+    back = shard_in[None]
+    for s in range(k_all.bit_length() - 1):
+        carry_out = 1 << s
+        arr_now = lax.ppermute(back, peer_axis, [(ix, ix ^ carry_out) for ix in range(k_all)])
+        passed = jnp.stack([back, arr_now])
+        big = lax.axis_index(peer_axis)
+        val = big >> s & 1
+        back = jnp.where(val == 0, passed, passed[::-1]).reshape(-1, *shard_in.shape)
+    return back
 
 
 def from_behind(value, axis, steps):
@@ -61,10 +82,15 @@
     query_cols = query_heads * HEAD_SIZE
     kv_cols = key_value_heads * HEAD_SIZE
     full_rows = lax.all_gather(tokens, "hid", axis=1, tiled=True)
+
+    def group_strings(target, xin, k_dim):
+        current_arr = see_clusters(target, xin)
+        return draw_islands_on(current_arr, k_dim)
+
     pieces = (
         lax.all_gather(w_query, "tok", axis=0, tiled=True),
         lax.all_gather(key_weight, "tok", axis=0, tiled=True),
-        lax.all_gather(value_weight, "tok", axis=0, tiled=True),
+        group_strings(value_weight, "tok", 0),
     )
     columns = full_rows
     query_unnormed = jnp.dot(columns, pieces[0], preferred_element_type=jnp.float32)

time: 535 us -> 507 us (0.948)
  waiting for transfers between devices: 328 us -> 280 us
  starting transfers between devices: 38.1 us -> 45.8 us
  other arithmetic: 25.4 us -> 31.7 us
  matrix products: 63.2 us -> 69.4 us
    all_gather x1, waiting for transfers between devices: 57.2 us -> 18 us  [local(): full_rows = lax.all_gather(tokens, 'hid', axis=1, tiled=True)]
    ppermute x0 -> x2, waiting for transfers between devices: none -> 31.1 us  [see_clusters(): lax.ppermute(back, peer_axis, [(ix, ix ^ carry_out) for ix in range(k_all)])]
    all_gather x1, waiting for transfers between devices: 20.9 us -> 0.01 us  [local(): lax.all_gather(value_weight, 'tok', axis=0, tiled=True)]
    all_gather x1, waiting for transfers between devices: 29.4 us -> 18.4 us  [local(): lax.all_gather(w_query, 'tok', axis=0, tiled=True)]
    ppermute x8, waiting for transfers between devices: 28.1 us -> 21.8 us  [from_behind(): lax.ppermute(value, axis, [(source, source + steps) for source in range(f...]
  transfers between devices with their start and end apart: 18 -> 20, of which waited for: 16 -> 16; matrix products, arithmetic and copies ran while one was open for 24% -> 28% of each run, Pallas kernels for 0% -> 0%
where the time goes in v1:
time: 507 us; the launch traced here: 505 us
  waiting for transfers between devices  280 us (55%)
  matrix products  69.4 us (14%)
  local copies, waits for them, and re-layouts  62.6 us (12%)
  starting transfers between devices  45.8 us (9%)
  other arithmetic  31.7 us (6%)
  between operations  14.9 us (3%)
    unnamed x11, waiting for transfers between devices  78.1 us
    ppermute x8, starting transfers between devices, from_behind(): lax.ppermute(value, axis, [(source, source + steps) for source in range(f...  41.4 us
    unnamed x90, local copies, waits for them, and re-layouts  40.8 us
    reduce_scatter x1, waiting for transfers between devices, local(): lax.psum_scatter(block_rows.astype(jnp.bfloat16), 'hid', scatter_dimensio...  38.4 us
    ppermute x2, waiting for transfers between devices, see_clusters(): lax.ppermute(back, peer_axis, [(ix, ix ^ carry_out) for ix in range(k_all)])  31.1 us
    all_gather x1, waiting for transfers between devices, local(): lax.all_gather(key_weight, 'tok', axis=0, tiled=True)  26.6 us
    all_gather x1, waiting for transfers between devices, local(): all_heads = lax.all_gather(attended, 'hid', axis=1, tiled=True)  25.9 us
    reduce_scatter x1, waiting for transfers between devices, local(): lax.psum_scatter(partial_heads.astype(jnp.bfloat16), 'hid', scatter_dimen...  22.1 us
  transfers between devices with their start and end apart: 20, of which 16 were waited for; matrix products, arithmetic and copies ran while one was open for 28% of the time, Pallas kernels for 0%

profile of v1, /device:TPU:0, one launch (start us, length us, event | category | flops | bytes accessed | tf_op | source)
XLA Modules:
  0.0 504.8 jit_solution(6852873090450270514)
XLA Ops:
  18.2 29.4 %collective-permute-done.1 = bf16[2,1344,256]{2,1,0:T(8,128)(2,1)} collective-permute-done((bf16[2,1344,256]{2,1,0:T(8,128)(2,1)}, bf16[2,1344,256]{2,1,0:T(8,128)(2,1)}, u32[]{:S(2)}, u32[]{:S(2)}) %collective-permute-start.1) | collective-permute-done | bytes 1376288 | tf_op jit(solution)/shard_map/ppermute | solution.py:29
  51.3 18.0 %all-gather.7.cloned.1.call-done = bf16[256,5376]{0,1:T(8,128)(2,1)} async-done(((bf16[256,1344]{0,1:T(8,128)(2,1)}), bf16[256,5376]{0,1:T(8,128)(2,1)}) %all-gather.7.cloned.1.call-update) | async-done | bytes 2752528 | tf_op jit(solution)/shard_map/all_gather | solution.py:84
  69.3 26.6 %all-gather.9.cloned.1.call-done = bf16[5376,256]{1,0:T(8,128)(2,1)} async-done(((bf16[1344,256]{1,0:T(8,128)(2,1)}), bf16[5376,256]{1,0:T(8,128)(2,1)}) %all-gather.9.cloned.1.call-update) | async-done | bytes 2752528 | tf_op jit(solution)/shard_map/all_gather | solution.py:92
  95.9 3.8 multiply_reduce_fusion.3
  103.0 3.3 fusion.17
  110.9 10.3 %collective-permute-start.3 = (bf16[2,256,256]{2,1,0:T(8,128)(2,1)S(1)}, bf16[2,256,256]{2,1,0:T(8,128)(2,1)}, u32[]{:S(2)}, u32[]{:S(2)}) collective-permute-start(bf16[2,256,256]{2,1,0:T(8,128)(2,1)S(1)} %collective-permute-done.2), channel_id=1, source_target_pairs={{0,4},{4,8},{8,12},{1,5},{5,9},{9,13},{2,6},{6,10},{10,14},{3,7},{... | collective-permute-start | bytes 786440 | tf_op jit(solution)/shard_map/ppermute | solution.py:40
  121.8 12.7 %collective-permute-start.4 = (bf16[2,256,256]{2,1,0:T(8,128)(2,1)}, bf16[2,256,256]{2,1,0:T(8,128)(2,1)}, u32[]{:S(2)}, u32[]{:S(2)}) collective-permute-start(bf16[2,256,256]{2,1,0:T(8,128)(2,1)} %collective-permute-done.3), channel_id=1, source_target_pairs={{0,4},{4,8},{8,12},{1,5},{5,9},{9,13},{2,6},{6,10},{10,14},{3,7},{... | collective-permute-start | bytes 786440 | tf_op jit(solution)/shard_map/ppermute | solution.py:40
  135.3 10.9 %collective-permute-start.5 = (bf16[2,256,256]{2,1,0:T(8,128)(2,1)}, bf16[2,256,256]{2,1,0:T(8,128)(2,1)S(1)}, u32[]{:S(2)}, u32[]{:S(2)}) collective-permute-start(bf16[2,256,256]{2,1,0:T(8,128)(2,1)} %collective-permute-done.4), channel_id=1, source_target_pairs={{0,4},{4,8},{8,12},{1,5},{5,9},{9,13},{2,6},{6,10},{10,14},{3,7},{... | collective-permute-start | bytes 786440 | tf_op jit(solution)/shard_map/ppermute | solution.py:40
  154.0 6.0 %convolution_convert_fusion.3 = bf16[256,2048]{1,0:T(8,128)(2,1)} fusion(bf16[256,1344]{0,1:T(8,128)(2,1)S(1)} %copy-done, bf16[2048,1344]{0,1:T(8,128)(2,1)} %all-gather.15.cloned.1.call-done), kind=kOutput, calls=%fused_computation.25 | convolution fusion | flops 1409810432 | bytes 7241728 | tf_op jit(solution)/shard_map/td,hd->th/dot_general | solution.py:151
  172.3 18.4 %all-gather.11.cloned.1.call-done = bf16[5376,512]{1,0:T(8,128)(2,1)} async-done(((bf16[1344,512]{1,0:T(8,128)(2,1)}), bf16[5376,512]{1,0:T(8,128)(2,1)}) %all-gather.11.cloned.1.call-update) | async-done | bytes 5505040 | tf_op jit(solution)/shard_map/all_gather | solution.py:91
  190.8 5.0 fusion.55
  198.6 22.1 %reduce-scatter.7.cloned.1.call-done = bf16[256,512]{1,0:T(8,128)(2,1)} async-done(((bf16[256,2048]{1,0:T(8,128)(2,1)}), bf16[256,512]{1,0:T(8,128)(2,1)}) %reduce-scatter.7.cloned.1.call-update) | async-done | bytes 262160 | tf_op jit(solution)/shard_map/reduce_scatter | solution.py:157
  225.0 7.2 %fusion.2 = (f32[2,2,256]{2,1,0:T(2,128)S(1)}, f32[2,2,256,1280]{2,3,1,0:T(8,128)}) fusion(f32[2,1280,256,2]{2,1,3,0:T(8,128)} %fusion.21, bf16[1280,2,128,1]{0,2,3,1:T(8,128)(2,1)S(1)} %copy-done.14, pred[256,1280]{0,1:T(8,128)(4,1)S(1)} %copy-done.34, bf16[256,2,2,64]{3,0,2,1:T(8,128)(2,1)S(1)} %bitcast.117, bf16[256,2,2,64]{3,0,2,1:T(8,128)(2,1)S(1)} %bitcast.119), kind=kOutput, calls=%fused_computation.8 | convolution fusion | flops 342623488 | bytes 11735040 | tf_op jit(solution)/shard_map/div | solution.py:137
  232.2 3.8 fusion.14
  236.8 25.9 %all-gather.13.cloned.1.call-done = bf16[256,2048]{0,1:T(8,128)(2,1)} async-done(((bf16[256,512]{0,1:T(8,128)(2,1)}), bf16[256,2048]{0,1:T(8,128)(2,1)}) %all-gather.13.cloned.1.call-update) | async-done | bytes 1048592 | tf_op jit(solution)/shard_map/all_gather | solution.py:143
  262.7 5.3 %convolution_convert_fusion.1 = bf16[2048,1344]{0,1:T(8,128)(2,1)} fusion(bf16[256,2048]{0,1:T(8,128)(2,1)} %all-gather.13.cloned.1.call-done, bf16[256,1344]{0,1:T(8,128)(2,1)S(1)} %copy-done), kind=kOutput, calls=%fused_computation.5 | convolution fusion | flops 1412038656 | bytes 7241728 | tf_op jit(solution)/shard_map/th,td->hd/dot_general | solution.py:163
  268.2 5.7 %fusion.4 = bf16[2,2,256,1280]{2,3,1,0:T(8,128)(2,1)S(1)} fusion(f32[2,1280,256,2]{2,1,3,0:T(8,128)} %fusion.21, f32[2,2,256,1280]{2,3,1,0:T(8,128)} %get-tuple-element.53, f32[2,2,256]{2,1,0:T(2,128)S(1)} %get-tuple-element.52), kind=kLoop, calls=%fused_computation.10 | loop fusion | flops 5242880 | bytes 13111296 | tf_op jit(solution)/shard_map/convert_element_type | solution.py:178
  275.0 3.5 fusion.7
  286.8 8.9 %collective-permute-done.7 = bf16[2,256,256]{1,2,0:T(8,128)(2,1)} collective-permute-done((bf16[2,256,256]{1,2,0:T(8,128)(2,1)}, bf16[2,256,256]{1,2,0:T(8,128)(2,1)}, u32[]{:S(2)}, u32[]{:S(2)}) %collective-permute-start.7) | collective-permute-done | bytes 262176 | tf_op jit(solution)/shard_map/ppermute | solution.py:40
  300.7 5.0 collective-permute-done.8
  311.7 3.4 collective-permute-done.9
  318.8 7.7 %fusion = bf16[5376,1024]{0,1:T(8,128)(2,1)} fusion(bf16[256,5376]{0,1:T(8,128)(2,1)} %all-gather.7.cloned.1.call-done, bf16[256,256]{1,0:T(8,128)(2,1)S(1)} %copy.109, bf16[256,256]{1,0:T(8,128)(2,1)S(1)} %copy.108, bf16[256,512]{1,0:T(8,128)(2,1)S(1)} %bitcast.116), kind=kOutput, calls=%fused_computation.1 | convolution fusion | flops 2825650176 | bytes 14286848 | tf_op jit(solution)/shard_map/td,tc->dc/dot_general | solution.py:234
  326.5 14.7 %copy.133 = bf16[5376,1024]{1,0:T(8,128)(2,1)} copy(bf16[5376,1024]{0,1:T(8,128)(2,1)} %fusion) | data formatting | bytes 22020096
  342.2 4.5 fusion.49
  346.7 3.2 convolution_add_fusion.1
  349.9 5.9 %fusion.1 = bf16[256,5376]{0,1:T(8,128)(2,1)} fusion(f32[256,5376]{0,1:T(8,128)} %convolution_add_fusion.1, bf16[5376,256]{1,0:T(8,128)(2,1)} %all-gather.17.cloned.1.call-done, f32[2,256,256]{1,2,0:T(8,128)S(1)} %copy-done.13), kind=kOutput, calls=%fused_computation.4 | convolution fusion | flops 707395584 | bytes 11141120 | tf_op jit(solution)/shard_map/tc,dc->td/dot_general | solution.py:225
  357.1 5.6 %convolution_convert_fusion.2 = bf16[256,1344]{0,1:T(8,128)(2,1)} fusion(bf16[2048,1344]{0,1:T(8,128)(2,1)} %all-gather.15.cloned.1.call-done, bf16[256,2048]{0,1:T(8,128)(2,1)S(1)} %copy-done.26), kind=kOutput, calls=%fused_computation.24 | convolution fusion | flops 1409630208 | bytes 7241728 | tf_op jit(solution)/shard_map/dot_general | solution.py:145
  362.7 3.6 convert_element_type.115
  366.4 74.7 %reduce-scatter.13.cloned.1.call-done = bf16[1344,1024]{1,0:T(8,128)(2,1)} async-done(((bf16[5376,1024]{1,0:T(8,128)(2,1)}), bf16[1344,1024]{1,0:T(8,128)(2,1)}) %reduce-scatter.13.cloned.1.call-update) | async-done | bytes 2752528
  441.1 4.6 copy.134
  448.8 3.8 copy.110
  459.6 38.4 %reduce-scatter.9.cloned.1.call-done = bf16[256,1344]{0,1:T(8,128)(2,1)} async-done(((bf16[256,5376]{0,1:T(8,128)(2,1)}), bf16[256,1344]{0,1:T(8,128)(2,1)}) %reduce-scatter.9.cloned.1.call-update) | async-done | bytes 688144 | tf_op jit(solution)/shard_map/reduce_scatter | solution.py:228
  (181 shorter events, 88.0 us)
Async XLA Ops:
  7.2 146.9 %copy-start = (bf16[256,1344]{0,1:T(8,128)(2,1)S(1)}, bf16[256,1344]{0,1:T(8,128)(2,1)}, u32[]{:S(2)}) copy-start(bf16[256,1344]{0,1:T(8,128)(2,1)} %param.17) | copy-start | bytes 2064388
  7.2 62.1 %all-gather.7.cloned.1.call-start = ((), (), s32[]{:S(2)}) async-start(), calls=%async_computation.4 | async-start | bytes 3440640 | tf_op jit(solution)/shard_map/all_gather | solution.py:84
  7.9 88.0 %all-gather.9.cloned.1.call-start = ((), (), s32[]{:S(2)}) async-start(), calls=%async_computation.5 | async-start | bytes 3440640 | tf_op jit(solution)/shard_map/all_gather | solution.py:92
  8.7 145.3 %all-gather.15.cloned.1.call-start = ((), (), s32[]{:S(2)}) async-start(), calls=%async_computation.8 | async-start | bytes 6881280 | tf_op jit(solution)/shard_map/all_gather | solution.py:147
  9.4 181.3 %all-gather.11.cloned.1.call-start = ((), (), s32[]{:S(2)}) async-start(), calls=%async_computation.6 | async-start | bytes 6881280 | tf_op jit(solution)/shard_map/all_gather | solution.py:91
  10.0 210.7 %reduce-scatter.7.cloned.1.call-start = ((), (), s32[]{:S(2)}) async-start(), calls=%async_computation.9 | async-start | bytes 1310720 | tf_op jit(solution)/shard_map/reduce_scatter | solution.py:157
  10.0 2.3 collective-permute-start
  13.9 33.7 %collective-permute-start.1 = (bf16[2,1344,256]{2,1,0:T(8,128)(2,1)}, bf16[2,1344,256]{2,1,0:T(8,128)(2,1)}, u32[]{:S(2)}, u32[]{:S(2)}) collective-permute-start(bf16[2,1344,256]{2,1,0:T(8,128)(2,1)} %get-tuple-element.35), channel_id=1, source_target_pairs={{0,8},{4,12},{8,0},{12,4},{1,9},{5,13},{9,1},{13,5},{2,10},{6,14},... | collective-permute-start | bytes 4128776 | tf_op jit(solution)/shard_map/ppermute | solution.py:29
  17.4 31.8 %copy-start.19 = (f32[256,64]{1,0:T(8,128)}, f32[256,64]{1,0:T(8,128)S(1)}, u32[]{:S(2)}) copy-start(f32[256,64]{1,0:T(8,128)S(1)} %get-tuple-element.48) | copy-start | bytes 196612
  17.4 31.8 %copy-start.21 = (f32[256,64]{1,0:T(8,128)}, f32[256,64]{1,0:T(8,128)S(1)}, u32[]{:S(2)}) copy-start(f32[256,64]{1,0:T(8,128)S(1)} %get-tuple-element.49) | copy-start | bytes 196612
  51.3 49.2 %copy-start.38 = (f32[128]{0:T(128)S(1)}, f32[128]{0:T(128)}, u32[]{:S(2)}) copy-start(f32[128]{0:T(128)} %param.15) | copy-start | bytes 1540
  69.3 33.6 %copy-start.2 = (bf16[256,5376]{0,1:T(8,128)(2,1)S(1)}, bf16[256,5376]{0,1:T(8,128)(2,1)}, u32[]{:S(2)}) copy-start(bf16[256,5376]{0,1:T(8,128)(2,1)} %all-gather.7.cloned.1.call-done) | copy-start | bytes 8257540
  106.9 3.3 collective-permute-start.2
  110.9 10.9 %collective-permute-start.3 = (bf16[2,256,256]{2,1,0:T(8,128)(2,1)S(1)}, bf16[2,256,256]{2,1,0:T(8,128)(2,1)}, u32[]{:S(2)}, u32[]{:S(2)}) collective-permute-start(bf16[2,256,256]{2,1,0:T(8,128)(2,1)S(1)} %collective-permute-done.2), channel_id=1, source_target_pairs={{0,4},{4,8},{8,12},{1,5},{5,9},{9,13},{2,6},{6,10},{10,14},{3,7},{... | collective-permute-start | bytes 786440 | tf_op jit(solution)/shard_map/ppermute | solution.py:40
  121.8 13.5 %collective-permute-start.4 = (bf16[2,256,256]{2,1,0:T(8,128)(2,1)}, bf16[2,256,256]{2,1,0:T(8,128)(2,1)}, u32[]{:S(2)}, u32[]{:S(2)}) collective-permute-start(bf16[2,256,256]{2,1,0:T(8,128)(2,1)} %collective-permute-done.3), channel_id=1, source_target_pairs={{0,4},{4,8},{8,12},{1,5},{5,9},{9,13},{2,6},{6,10},{10,14},{3,7},{... | collective-permute-start | bytes 786440 | tf_op jit(solution)/shard_map/ppermute | solution.py:40
  135.3 13.0 %collective-permute-start.5 = (bf16[2,256,256]{2,1,0:T(8,128)(2,1)}, bf16[2,256,256]{2,1,0:T(8,128)(2,1)S(1)}, u32[]{:S(2)}, u32[]{:S(2)}) collective-permute-start(bf16[2,256,256]{2,1,0:T(8,128)(2,1)} %collective-permute-done.4), channel_id=1, source_target_pairs={{0,4},{4,8},{8,12},{1,5},{5,9},{9,13},{2,6},{6,10},{10,14},{3,7},{... | collective-permute-start | bytes 786440 | tf_op jit(solution)/shard_map/ppermute | solution.py:40
  160.0 102.7 %all-gather.13.cloned.1.call-start = ((), (), s32[]{:S(2)}) async-start(), calls=%async_computation.7 | async-start | bytes 1310720 | tf_op jit(solution)/shard_map/all_gather | solution.py:143
  172.3 25.3 %copy-start.37 = (f32[128]{0:T(128)S(1)}, f32[128]{0:T(128)}, u32[]{:S(2)}) copy-start(f32[128]{0:T(128)} %param.14) | copy-start | bytes 1540
  197.0 24.8 %copy-start.3 = (f32[256,4,128]{2,1,0:T(4,128)}, f32[256,4,128]{2,1,0:T(4,128)S(1)}, u32[]{:S(2)}) copy-start(f32[256,4,128]{2,1,0:T(4,128)S(1)} %reshape.228) | copy-start | bytes 1572868
  197.0 24.8 %copy-start.6 = (bf16[1280,2,128]{2,1,0:T(2,128)(2,1)S(1)}, bf16[1280,2,128]{2,1,0:T(2,128)(2,1)}, u32[]{:S(2)}) copy-start(bf16[1280,2,128]{2,1,0:T(2,128)(2,1)} %reshape_squeeze.9) | copy-start | bytes 1966084
  197.6 24.2 %copy-start.27 = (f32[256,4]{1,0:T(8,128)}, f32[256,4]{1,0:T(8,128)S(1)}, u32[]{:S(2)}) copy-start(f32[256,4]{1,0:T(8,128)S(1)} %copy.90) | copy-start | bytes 12292
  236.0 113.9 %all-gather.17.cloned.1.call-start = ((), (), s32[]{:S(2)}) async-start(), calls=%async_computation.10 | async-start | bytes 3440640 | tf_op jit(solution)/shard_map/all_gather | solution.py:219
  236.7 126.0 %reduce-scatter.11.cloned.1.call-start = ((), (), s32[]{:S(2)}) async-start(), calls=%async_computation.12 | async-start | bytes 6881280 | tf_op jit(solution)/shard_map/reduce_scatter | solution.py:162
  268.0 173.1 %reduce-scatter.13.cloned.1.call-start = ((), (), s32[]{:S(2)}) async-start(), calls=%async_computation.13 | async-start | bytes 13762560
  278.6 3.6 collective-permute-start.6
  282.9 12.7 %collective-permute-start.7 = (bf16[2,256,256]{1,2,0:T(8,128)(2,1)}, bf16[2,256,256]{1,2,0:T(8,128)(2,1)}, u32[]{:S(2)}, u32[]{:S(2)}) collective-permute-start(bf16[2,256,256]{1,2,0:T(8,128)(2,1)} %fusion.31), channel_id=1, source_target_pairs={{4,0},{8,4},{12,8},{5,1},{9,5},{13,9},{6,2},{10,6},{14,10},{7,3},{... | collective-permute-start | bytes 786440 | tf_op jit(solution)/shard_map/ppermute | solution.py:40
  284.7 13.9 %copy-start.23 = (f32[256,64]{1,0:T(8,128)S(1)}, f32[256,64]{1,0:T(8,128)}, u32[]{:S(2)}) copy-start(f32[256,64]{1,0:T(8,128)} %copy-done.21) | copy-start | bytes 196612
  286.8 13.2 %copy-start.4 = (f32[256,4,128]{2,1,0:T(4,128)S(1)}, f32[256,4,128]{2,1,0:T(4,128)}, u32[]{:S(2)}) copy-start(f32[256,4,128]{2,1,0:T(4,128)} %copy-done.3) | copy-start | bytes 1572868
  297.4 8.4 %collective-permute-start.8 = (bf16[2,256,256]{1,2,0:T(8,128)(2,1)}, bf16[2,256,256]{1,2,0:T(8,128)(2,1)}, u32[]{:S(2)}, u32[]{:S(2)}) collective-permute-start(bf16[2,256,256]{1,2,0:T(8,128)(2,1)} %fusion.34), channel_id=1, source_target_pairs={{4,0},{8,4},{12,8},{5,1},{9,5},{13,9},{6,2},{10,6},{14,10},{7,3},{... | collective-permute-start | bytes 786440 | tf_op jit(solution)/shard_map/ppermute | solution.py:40
  307.5 7.6 %collective-permute-start.9 = (bf16[2,256,256]{1,2,0:T(8,128)(2,1)}, bf16[2,256,256]{1,2,0:T(8,128)(2,1)}, u32[]{:S(2)}, u32[]{:S(2)}) collective-permute-start(bf16[2,256,256]{1,2,0:T(8,128)(2,1)} %fusion.26), channel_id=1, source_target_pairs={{4,0},{8,4},{12,8},{5,1},{9,5},{13,9},{6,2},{10,6},{14,10},{7,3},{... | collective-permute-start | bytes 786440 | tf_op jit(solution)/shard_map/ppermute | solution.py:40
  341.3 156.7 %reduce-scatter.9.cloned.1.call-start = ((), (), s32[]{:S(2)}) async-start(), calls=%async_computation.11 | async-start | bytes 3440640 | tf_op jit(solution)/shard_map/reduce_scatter | solution.py:228
  455.2 42.8 %copy-start.1 = (bf16[256,1344]{0,1:T(8,128)(2,1)S(1)}, bf16[256,1344]{0,1:T(8,128)(2,1)}, u32[]{:S(2)}) copy-start(bf16[256,1344]{0,1:T(8,128)(2,1)} %param.17) | copy-start | bytes 2064388
  (27 other events, 106.8 us)
Sparse Core Ops, SparseCore 0:
  9.6 59.6 all-gather.6
  70.9 25.0 all-gather.8
  97.5 46.0 all-gather.14
  145.0 45.7 all-gather.10
  193.5 27.1 reduce-scatter.6
  236.1 26.5 all-gather.12
  264.3 28.5 all-gather.16
  295.6 55.3 reduce-scatter.10
  353.6 87.4 reduce-scatter.12
  443.8 54.1 reduce-scatter.8
